TPU v7x, 512 devices: a whole 4x8x8 slice. The times are simulated.
512 devices in a mesh: row: 8 (over z), col: 16 (over y, core), depth: 4 (over x).
Axes of the slice: x: 4, y: 8, z: 8, core: 2. Of those that a mesh axis runs over, the one named last changes fastest.
Arguments:
- tokens: bfloat16 [4096, 8192], P(('row', 'col'), 'depth'), may hold values from -6 to 6
- gate_weight: bfloat16 [8192, 14336], P(('depth', 'row'), 'col'), may hold values from -0.0625 to 0.0625
- up_weight: bfloat16 [8192, 14336], P(('depth', 'row'), 'col'), may hold values from -0.0625 to 0.0625
- down_weight: bfloat16 [14336, 8192], P(('col', 'row'), 'depth'), may hold values from -0.125 to 0.125
- gate_keep: int32 [64, 112], replicated, may hold values from 0 to 1, as said below
- up_keep: int32 [64, 112], replicated, may hold values from 0 to 1, as said below
- down_keep: int32 [112, 64], replicated, may hold values from 0 to 1, as said below
Outputs:
- mixed: bfloat16 [4096, 8192], P(('row', 'col'), 'depth')
Inputs may be any that keep to these rules, and one draw needn't show every extreme that they name: `gate_keep`: 1 marks a kept block of the gate projection, 0 a dropped one. `up_keep`: 1 marks a kept block of the up projection, 0 a dropped one. `down_keep`: 1 marks a kept block of the down projection, 0 a dropped one.
All inputs are finite; a program needn't handle non-finite values.
Results may differ from a plain program's by a relative error of at most 0.005.
Values may be sent and summed in bfloat16 or wider, within the bound.
No kernel may reach another device: no remote copies, remote signals or barrier semaphores. Data moves between devices by JAX's collectives and lax.ppermute only.
A program may use at most 64 MiB of HBM per device.

v0:
```python
import jax
import jax.numpy as jnp
from jax import lax
from jax.sharding import PartitionSpec as P

BLOCK = 128


def keep_table(keep, row_start, col_start, row_count, col_count):
    keep_bits = keep.astype(jnp.bfloat16)
    row_ids = (row_start + jnp.arange(row_count, dtype=jnp.int32)) // BLOCK
    col_ids = (col_start + jnp.arange(col_count, dtype=jnp.int32)) // BLOCK
    pick_rows = (row_ids[:, None] == jnp.arange(keep.shape[0], dtype=jnp.int32)[None, :]).astype(
        jnp.bfloat16
    )
    pick_cols = (jnp.arange(keep.shape[1], dtype=jnp.int32)[:, None] == col_ids[None, :]).astype(
        jnp.bfloat16
    )
    inner = jnp.dot(keep_bits, pick_cols, preferred_element_type=jnp.float32).astype(jnp.bfloat16)
    return jnp.dot(pick_rows, inner, preferred_element_type=jnp.float32).astype(jnp.bfloat16)


def add_panel(token_block, piece):
    return jnp.dot(token_block, piece, preferred_element_type=jnp.float32)


def on_device(tokens, gate_weight, up_weight, down_weight, gate_keep, up_keep, down_keep):
    depth_pos = lax.axis_index("depth")
    row_pos = lax.axis_index("row")
    column_pos = lax.axis_index("col")
    row_total = lax.axis_size("row")
    feature_rows = gate_weight.shape[0]
    hidden_cols = gate_weight.shape[1]
    feature_start = (depth_pos * row_total + row_pos) * feature_rows
    hidden_start = column_pos * hidden_cols
    gate_masked = gate_weight * keep_table(
        gate_keep, feature_start, hidden_start, feature_rows, hidden_cols
    )
    up_masked = up_weight * keep_table(
        up_keep, feature_start, hidden_start, feature_rows, hidden_cols
    )
    down_rows_count = down_weight.shape[0]
    down_features = down_weight.shape[1]
    down_start = (column_pos * row_total + row_pos) * down_rows_count
    down_masked = down_weight * keep_table(
        down_keep, down_start, depth_pos * down_features, down_rows_count, down_features
    )
    token_block = lax.all_gather(tokens, "col", axis=0, tiled=True)

    def add_one(piece):
        return add_panel(token_block, piece)

    gate = add_one(lax.all_gather(gate_masked, "row", axis=0, tiled=True))
    up = add_one(lax.all_gather(up_masked, "row", axis=0, tiled=True))
    both = jnp.stack((gate, up), 0)
    total = lax.psum(both, "depth")
    hidden = (jax.nn.silu(total[0]) * total[1]).astype(jnp.bfloat16)
    down_block = lax.all_gather(down_masked, "row", axis=0, tiled=True)
    mixed = lax.psum_scatter(
        jnp.dot(hidden, down_block, preferred_element_type=jnp.float32),
        "col",
        scatter_dimension=0,
        tiled=True,
    )
    return mixed.astype(jnp.bfloat16)


def solution(mesh):
    placed = (
        P(("row", "col"), "depth"),
        P(("depth", "row"), "col"),
        P(("depth", "row"), "col"),
        P(("col", "row"), "depth"),
        P(),
        P(),
        P(),
    )
    return jax.shard_map(
        on_device, mesh=mesh, in_specs=placed, out_specs=P(("row", "col"), "depth"), check_vma=False
    )
```

profile of v0, /device:TPU:25, one launch (start us, length us, event | category | flops | bytes accessed | tf_op | source)
XLA Modules:
  0.0 393.9 jit_solution(8674119538249657588)
XLA Ops:
  6.5 0.0 copy-start
  6.5 0.0 copy-start.1
  6.5 0.0 all-gather.7.cloned.1.call-start
  6.5 0.7 all-gather.7.cloned.1.call-update
  7.3 0.0 all-gather.9.cloned.1.call-start
  7.4 2.3 fusion.4
  9.7 0.0 all-gather.9.cloned.1.call-update
  9.7 0.0 all-gather.5.cloned.1.call-start
  9.8 2.3 fusion.3
  12.1 0.0 all-gather.5.cloned.1.call-update
  12.1 0.0 all-gather.11.cloned.1.call-start
  12.2 0.0 copy-done
  12.2 0.0 copy-done.1
  12.2 1.4 fusion
  13.7 0.0 all-gather.11.cloned.1.call-update
  13.7 0.0 all-reduce.2.cloned.1.call-start
  13.7 42.2 %all-gather.7.cloned.1.call-done = bf16[512,2048]{1,0:T(8,128)(2,1)} async-done(((bf16[32,2048]{1,0:T(8,128)(2,1)}), bf16[512,2048]{1,0:T(8,128)(2,1)}) %all-gather.7.cloned.1.call-update) | async-done | bytes 2097168 | tf_op jit(solution)/shard_map/all_gather | solution.py:48
  55.9 54.2 %all-gather.9.cloned.1.call-done = bf16[2048,896]{1,0:T(8,128)(2,1)} async-done(((bf16[256,896]{1,0:T(8,128)(2,1)}), bf16[2048,896]{1,0:T(8,128)(2,1)}) %all-gather.9.cloned.1.call-update) | async-done | bytes 3670032 | tf_op jit(solution)/shard_map/all_gather | solution.py:54
  110.2 4.8 %convolution_bitcast_fusion = f32[1,512,896]{1,2,0:T(8,128)S(1)} fusion(bf16[2048,896]{1,0:T(8,128)(2,1)} %all-gather.9.cloned.1.call-done, bf16[512,2048]{1,0:T(8,128)(2,1)} %all-gather.7.cloned.1.call-done), kind=kOutput, calls=%fused_computation.8 | convolution fusion | flops 1879048192 | bytes 7602176 | tf_op jit(solution)/shard_map/dot_general | solution.py:24
  115.0 48.7 %all-gather.5.cloned.1.call-done = bf16[2048,896]{1,0:T(8,128)(2,1)} async-done(((bf16[256,896]{1,0:T(8,128)(2,1)}), bf16[2048,896]{1,0:T(8,128)(2,1)}) %all-gather.5.cloned.1.call-update) | async-done | bytes 3670032 | tf_op jit(solution)/shard_map/all_gather | solution.py:53
  163.7 4.8 %convolution_bitcast_fusion.1 = f32[1,512,896]{1,2,0:T(8,128)S(1)} fusion(bf16[2048,896]{1,0:T(8,128)(2,1)} %all-gather.5.cloned.1.call-done, bf16[512,2048]{1,0:T(8,128)(2,1)} %all-gather.7.cloned.1.call-done), kind=kOutput, calls=%fused_computation.9 | convolution fusion | flops 1879048192 | bytes 7602176 | tf_op jit(solution)/shard_map/dot_general | solution.py:24
  168.5 2.3 pad_maximum_fusion
  170.8 0.0 all-reduce.2.cloned.1.call-update
  170.9 0.0 reduce-scatter.2.cloned.1.call-start
  170.9 46.2 %all-gather.11.cloned.1.call-done = bf16[896,2048]{1,0:T(8,128)(2,1)} async-done(((bf16[112,2048]{1,0:T(8,128)(2,1)}), bf16[896,2048]{1,0:T(8,128)(2,1)}) %all-gather.11.cloned.1.call-update) | async-done | bytes 3670032 | tf_op jit(solution)/shard_map/all_gather | solution.py:58
  217.1 95.3 %all-reduce.2.cloned.1.call-done = f32[2,512,896]{1,2,0:T(8,128)} async-done(((f32[2,512,896]{1,2,0:T(8,128)}), f32[2,512,896]{1,2,0:T(8,128)}) %all-reduce.2.cloned.1.call-update) | async-done | bytes 3670032 | tf_op jit(solution)/shard_map/psum | solution.py:56
  312.4 7.7 %fusion.5 = f32[512,2048]{1,0:T(8,128)} fusion(bf16[896,2048]{1,0:T(8,128)(2,1)} %all-gather.11.cloned.1.call-done, f32[2,512,896]{1,2,0:T(8,128)} %all-reduce.2.cloned.1.call-done), kind=kOutput, calls=%fused_computation.16 | convolution fusion | flops 1881800704 | bytes 11534336 | tf_op jit(solution)/shard_map/dot_general | solution.py:60
  320.0 0.0 reduce-scatter.2.cloned.1.call-update
  320.1 65.3 %reduce-scatter.2.cloned.1.call-done = f32[32,2048]{1,0:T(8,128)} async-done(((f32[512,2048]{1,0:T(8,128)}), f32[32,2048]{1,0:T(8,128)}) %reduce-scatter.2.cloned.1.call-update) | async-done | bytes 262160 | tf_op jit(solution)/shard_map/reduce_scatter | solution.py:59
  385.4 1.6 convert_element_type.52
  (4 shorter events, 0.0 us)
Async XLA Ops:
  6.5 5.7 %copy-start = (bf16[112,2048]{1,0:T(8,128)(2,1)S(1)}, bf16[112,2048]{1,0:T(8,128)(2,1)}, u32[]{:S(2)}) copy-start(bf16[112,2048]{1,0:T(8,128)(2,1)} %param.10) | copy-start | bytes 1376260
  6.5 5.7 %copy-start.1 = (s32[112,64]{0,1:T(8,128)S(1)}, s32[112,64]{0,1:T(8,128)}, u32[]{:S(2)}) copy-start(s32[112,64]{0,1:T(8,128)} %param.13) | copy-start | bytes 86020
  6.5 49.4 %all-gather.7.cloned.1.call-start = ((), (), s32[]{:S(2)}) async-start(), calls=%async_computation.2 | async-start | bytes 2228224 | tf_op jit(solution)/shard_map/all_gather | solution.py:48
  7.3 102.9 %all-gather.9.cloned.1.call-start = ((), (), s32[]{:S(2)}) async-start(), calls=%async_computation.3 | async-start | bytes 4128768 | tf_op jit(solution)/shard_map/all_gather | solution.py:54
  9.7 154.0 %all-gather.5.cloned.1.call-start = ((), (), s32[]{:S(2)}) async-start(), calls=%async_computation.1 | async-start | bytes 4128768 | tf_op jit(solution)/shard_map/all_gather | solution.py:53
  12.1 205.0 %all-gather.11.cloned.1.call-start = ((), (), s32[]{:S(2)}) async-start(), calls=%async_computation.5 | async-start | bytes 4128768 | tf_op jit(solution)/shard_map/all_gather | solution.py:58
  13.7 298.7 %all-reduce.2.cloned.1.call-start = ((), (), s32[]{:S(2)}) async-start(), calls=%async_computation.4 | async-start | bytes 7340032 | tf_op jit(solution)/shard_map/psum | solution.py:56
  170.9 214.5 %reduce-scatter.2.cloned.1.call-start = ((), (), s32[]{:S(2)}) async-start(), calls=%async_computation.6 | async-start | bytes 4456448 | tf_op jit(solution)/shard_map/reduce_scatter | solution.py:59
Sparse Core Ops, SparseCore 0:
  9.5 46.3 all-gather.6
  58.0 52.1 all-gather.8
  112.2 51.4 all-gather.4
  165.6 51.3 all-gather.10
  219.3 93.0 all-reduce.1
  320.2 65.1 reduce-scatter.1
where the time goes:
time: 394 us
  waiting for transfers between devices  353 us (90%)
  matrix products  23.4 us (6%)
  between operations  13.5 us (3%)
  other arithmetic  4 us (1%)
    psum x1, waiting for transfers between devices, on_device(): total = lax.psum(both, 'depth')  95.3 us
    reduce_scatter x1, waiting for transfers between devices, on_device(): lax.psum_scatter(jnp.dot(hidden, down_block, preferred_element_type=jnp.f...  65.3 us
    all_gather x1, waiting for transfers between devices, on_device(): up = add_one(lax.all_gather(up_masked, 'row', axis=0, tiled=True))  54.2 us
    all_gather x1, waiting for transfers between devices, on_device(): gate = add_one(lax.all_gather(gate_masked, 'row', axis=0, tiled=True))  48.7 us
    all_gather x1, waiting for transfers between devices, on_device(): down_block = lax.all_gather(down_masked, 'row', axis=0, tiled=True)  46.2 us
    all_gather x1, waiting for transfers between devices, on_device(): token_block = lax.all_gather(tokens, 'col', axis=0, tiled=True)  42.2 us
    dot_general x2, matrix products, add_panel(): return jnp.dot(token_block, piece, preferred_element_type=jnp.float32)  9.61 us
  transfers between devices with their start and end apart: 6, of which 6 were waited for; matrix products, arithmetic and copies ran while one was open for 5% of the time, Pallas kernels for 0%

commit v1 on v0

--- a/solution.py
+++ b/solution.py
@@ -4,6 +4,12 @@
 from jax.sharding import PartitionSpec as P
 
 BLOCK = 128
+
+
+def gather_and_add(shard, axis):
+    parts = lax.all_gather(shard, axis, axis=0, tiled=False)
+    summed = parts.sum(axis=0)
+    return summed
 
 
 def keep_table(keep, row_start, col_start, row_count, col_count):
@@ -53,7 +59,7 @@
     gate = add_one(lax.all_gather(gate_masked, "row", axis=0, tiled=True))
     up = add_one(lax.all_gather(up_masked, "row", axis=0, tiled=True))
     both = jnp.stack((gate, up), 0)
-    total = lax.psum(both, "depth")
+    total = gather_and_add(both, "depth")
     hidden = (jax.nn.silu(total[0]) * total[1]).astype(jnp.bfloat16)
     down_block = lax.all_gather(down_masked, "row", axis=0, tiled=True)
     mixed = lax.psum_scatter(

time: 394 us -> 452 us (1.15)
  the two profiles are of different devices: /device:TPU:25 before, /device:TPU:4 now
where the time goes in v1:
time: 452 us; the launch traced here: 451 us
  waiting for transfers between devices  388 us (86%)
  matrix products  23.3 us (5%)
  local copies, waits for them, and re-layouts  13.6 us (3%)
  between operations  13.5 us (3%)
  other arithmetic  12.1 us (3%)
    all_gather x1, waiting for transfers between devices, gather_and_add(): parts = lax.all_gather(shard, axis, axis=0, tiled=False)  137 us
    reduce_scatter x1, waiting for transfers between devices, on_device(): lax.psum_scatter(jnp.dot(hidden, down_block, preferred_element_type=jnp.f...  63.3 us
    all_gather x1, waiting for transfers between devices, on_device(): up = add_one(lax.all_gather(up_masked, 'row', axis=0, tiled=True))  54.4 us
    all_gather x1, waiting for transfers between devices, on_device(): gate = add_one(lax.all_gather(gate_masked, 'row', axis=0, tiled=True))  48.7 us
    all_gather x1, waiting for transfers between devices, on_device(): token_block = lax.all_gather(tokens, 'col', axis=0, tiled=True)  43.9 us
    all_gather x1, waiting for transfers between devices, on_device(): down_block = lax.all_gather(down_masked, 'row', axis=0, tiled=True)  40.3 us
    dot_general x2, matrix products, add_panel(): return jnp.dot(token_block, piece, preferred_element_type=jnp.float32)  9.61 us
  transfers between devices with their start and end apart: 6, of which 6 were waited for; matrix products, arithmetic and copies ran while one was open for 6% of the time, Pallas kernels for 0%

profile of v1, /device:TPU:4, one launch (start us, length us, event | category | flops | bytes accessed | tf_op | source)
XLA Modules:
  0.0 451.2 jit_solution(15507913701998366720)
XLA Ops:
  6.5 0.0 all-gather.9.cloned.1.call-start
  6.5 0.7 all-gather.9.cloned.1.call-update
  7.3 0.0 all-gather.11.cloned.1.call-start
  7.3 2.4 fusion.6
  9.7 0.0 all-gather.11.cloned.1.call-update
  9.7 0.0 all-gather.7.cloned.1.call-start
  9.8 2.3 fusion.5
  12.1 0.0 all-gather.7.cloned.1.call-update
  12.1 0.0 all-gather.15.cloned.1.call-start
  12.2 43.9 %all-gather.9.cloned.1.call-done = bf16[512,2048]{1,0:T(8,128)(2,1)} async-done(((bf16[32,2048]{1,0:T(8,128)(2,1)}), bf16[512,2048]{1,0:T(8,128)(2,1)}) %all-gather.9.cloned.1.call-update) | async-done | bytes 2097168 | tf_op jit(solution)/shard_map/all_gather | solution.py:54
  56.0 54.4 %all-gather.11.cloned.1.call-done = bf16[2048,896]{1,0:T(8,128)(2,1)} async-done(((bf16[256,896]{1,0:T(8,128)(2,1)}), bf16[2048,896]{1,0:T(8,128)(2,1)}) %all-gather.11.cloned.1.call-update) | async-done | bytes 3670032 | tf_op jit(solution)/shard_map/all_gather | solution.py:60
  110.4 4.8 %convolution_bitcast_fusion = f32[1,512,896]{1,2,0:T(8,128)S(1)} fusion(bf16[2048,896]{1,0:T(8,128)(2,1)} %all-gather.11.cloned.1.call-done, bf16[512,2048]{1,0:T(8,128)(2,1)} %all-gather.9.cloned.1.call-done), kind=kOutput, calls=%fused_computation.11 | convolution fusion | flops 1879048192 | bytes 7602176 | tf_op jit(solution)/shard_map/dot_general | solution.py:30
  115.2 48.7 %all-gather.7.cloned.1.call-done = bf16[2048,896]{1,0:T(8,128)(2,1)} async-done(((bf16[256,896]{1,0:T(8,128)(2,1)}), bf16[2048,896]{1,0:T(8,128)(2,1)}) %all-gather.7.cloned.1.call-update) | async-done | bytes 3670032 | tf_op jit(solution)/shard_map/all_gather | solution.py:59
  163.9 4.8 %convolution_bitcast_fusion.1 = f32[1,512,896]{1,2,0:T(8,128)S(1)} fusion(bf16[2048,896]{1,0:T(8,128)(2,1)} %all-gather.7.cloned.1.call-done, bf16[512,2048]{1,0:T(8,128)(2,1)} %all-gather.9.cloned.1.call-done), kind=kOutput, calls=%fused_computation.12 | convolution fusion | flops 1879048192 | bytes 7602176 | tf_op jit(solution)/shard_map/dot_general | solution.py:30
  168.7 2.2 pad_maximum_fusion
  170.9 4.6 %copy.8 = f32[2,512,896]{2,1,0:T(8,128)} copy(f32[2,512,896]{1,2,0:T(8,128)} %pad_maximum_fusion) | data formatting | bytes 7340032 | tf_op jit(solution)/shard_map/stack | solution.py:61
  175.6 0.0 copy-start
  175.6 0.0 copy-start.1
  175.6 0.0 all-gather.15.cloned.1.call-update
  175.6 0.0 all-gather.13.cloned.1.call-start
  175.7 0.9 copy-done
  176.6 0.0 copy-done.1
  176.6 1.5 fusion
  178.1 0.0 all-gather.13.cloned.1.call-update
  178.1 0.0 reduce-scatter.2.cloned.1.call-start
  178.1 137.1 %all-gather.15.cloned.1.call-done = f32[8,512,896]{2,1,0:T(8,128)} async-done(((f32[2,512,896]{2,1,0:T(8,128)}), f32[8,512,896]{2,1,0:T(8,128)}) %all-gather.15.cloned.1.call-update) | async-done | bytes 14680080 | tf_op jit(solution)/shard_map/all_gather | solution.py:10
  315.2 8.2 %reduce_sum.9 = f32[2,512,896]{2,1,0:T(8,128)} reduce(f32[4,2,512,896]{3,2,1,0:T(8,128)} %bitcast.33, f32[]{:T(128)} %constant.73.clone.1), dimensions={0}, to_apply=%region_0.1 | reduce | flops 2752512 | bytes 18350084 | tf_op jit(solution)/shard_map/reduce_sum | solution.py:11
  323.4 3.6 fusion.37
  327.0 2.8 copy.11
  329.8 1.7 copy.12
  331.5 40.3 %all-gather.13.cloned.1.call-done = bf16[896,2048]{1,0:T(8,128)(2,1)} async-done(((bf16[112,2048]{1,0:T(8,128)(2,1)}), bf16[896,2048]{1,0:T(8,128)(2,1)}) %all-gather.13.cloned.1.call-update) | async-done | bytes 3670032 | tf_op jit(solution)/shard_map/all_gather | solution.py:64
  371.8 7.6 %fusion.7 = f32[512,2048]{1,0:T(8,128)} fusion(bf16[896,2048]{1,0:T(8,128)(2,1)} %all-gather.13.cloned.1.call-done, f32[1,512,896]{1,2,0:T(8,128)} %copy.12, f32[1,512,896]{1,2,0:T(8,128)} %copy.11), kind=kOutput, calls=%fused_computation.19 | convolution fusion | flops 1881800704 | bytes 11534336 | tf_op jit(solution)/shard_map/dot_general | solution.py:66
  379.4 0.0 reduce-scatter.2.cloned.1.call-update
  379.4 63.3 %reduce-scatter.2.cloned.1.call-done = f32[32,2048]{1,0:T(8,128)} async-done(((f32[512,2048]{1,0:T(8,128)}), f32[32,2048]{1,0:T(8,128)}) %reduce-scatter.2.cloned.1.call-update) | async-done | bytes 262160 | tf_op jit(solution)/shard_map/reduce_scatter | solution.py:65
  442.8 1.6 convert_element_type.52
  (4 shorter events, 0.0 us)
Async XLA Ops:
  6.5 49.5 %all-gather.9.cloned.1.call-start = ((), (), s32[]{:S(2)}) async-start(), calls=%async_computation.2 | async-start | bytes 2228224 | tf_op jit(solution)/shard_map/all_gather | solution.py:54
  7.3 103.1 %all-gather.11.cloned.1.call-start = ((), (), s32[]{:S(2)}) async-start(), calls=%async_computation.3 | async-start | bytes 4128768 | tf_op jit(solution)/shard_map/all_gather | solution.py:60
  9.7 154.2 %all-gather.7.cloned.1.call-start = ((), (), s32[]{:S(2)}) async-start(), calls=%async_computation.1 | async-start | bytes 4128768 | tf_op jit(solution)/shard_map/all_gather | solution.py:59
  12.1 303.1 %all-gather.15.cloned.1.call-start = ((), (), s32[]{:S(2)}) async-start(), calls=%async_computation.6 | async-start | bytes 18350080 | tf_op jit(solution)/shard_map/all_gather | solution.py:10
  175.6 1.0 copy-start
  175.6 1.0 copy-start.1
  175.6 196.2 %all-gather.13.cloned.1.call-start = ((), (), s32[]{:S(2)}) async-start(), calls=%async_computation.4 | async-start | bytes 4128768 | tf_op jit(solution)/shard_map/all_gather | solution.py:64
  178.1 264.7 %reduce-scatter.2.cloned.1.call-start = ((), (), s32[]{:S(2)}) async-start(), calls=%async_computation.5 | async-start | bytes 4456448 | tf_op jit(solution)/shard_map/reduce_scatter | solution.py:65
Sparse Core Ops, SparseCore 0:
  9.5 46.5 all-gather.8
  58.1 52.2 all-gather.10
  112.5 51.3 all-gather.6
  175.7 139.4 all-gather.14
  317.1 54.6 all-gather.12
  379.5 63.1 reduce-scatter.1
